TPU v7x, 32 devices: a whole 2x2x4 slice. The times are simulated.
32 devices in a mesh: panel: 8 (over z, x), prb: 4 (over y, core).
Axes of the slice: x: 2, y: 2, z: 4, core: 2. Of those that a mesh axis runs over, the one named last changes fastest.
Arguments:
- channel: bfloat16 [112, 64, 64, 128], P('panel', 'prb'), may hold values from -0.1875 to 0.1875
- received: bfloat16 [112, 64, 64, 288], P('panel', 'prb'), may hold values from -6 to 6
- keep_list: int32 [112, 64, 3], P('panel', 'prb'), may hold values from 0 to 4, as said below
- alloc: int32 [64, 64], replicated, may hold values from 0 to 511, all different within a row
- noise_var: float32 [512], replicated, may hold values from 0.1 to 1
- owner: int32 [64, 64, 1], replicated, may hold values from 0 to 31; in each aligned block of 128 rows (0 to 127, 128 to 255, ..., all dimensions but the last counted through in order) at most 8 rows name the same one
Outputs:
- equalized: float32 [8192, 288], P(('panel', 'prb'))
Inputs may be any that keep to these rules, and one draw needn't show every extreme that they name: `keep_list`: entries below 4 name distinct beam blocks of the panel; entries equal to 4 are empty slots and stand after the kept ones; each panel keeps between 1 and 3 blocks for each PRB. `alloc`: each PRB lists 64 different users, and every user is listed by some PRB. Owners are device numbers along panel+prb. In each aligned block of 128 rows (PRB-major, then layer), no owner appears more than 8 times.
All inputs are finite; a program needn't handle non-finite values.
Results may differ from a plain program's by a relative error of at most 0.005.
Values may be sent and summed in bfloat16 or wider, within the bound.
A program may use at most 192 MiB of HBM per device.

v0:
```python
import math

import jax
import jax.numpy as jnp
from jax import lax
from jax.sharding import PartitionSpec as P

ANTENNA_EDGE = 8
NBLK = 4


def beamspace_tables(panel_side):
    length = panel_side * panel_side
    positions = jnp.arange(length, dtype=jnp.int32)
    first_axis = positions // panel_side
    second_axis = positions % panel_side
    phases = (
        first_axis[:, None] * first_axis[None, :] + second_axis[:, None] * second_axis[None, :]
    ) % panel_side
    angles = phases.astype(jnp.float32) * (2.0 * math.pi / panel_side)
    real_part = (jnp.cos(angles) / panel_side).astype(jnp.bfloat16)
    imag_part = (-jnp.sin(angles) / panel_side).astype(jnp.bfloat16)
    return (real_part, imag_part)


def combine_parts(first, second, width):
    return jnp.concatenate(
        [first[..., :width] - second[..., width:], second[..., :width] + first[..., width:]],
        axis=-1,
    ).astype(jnp.bfloat16)


def solve_one(factor_one, right_one):
    return jax.scipy.linalg.cho_solve((factor_one, True), right_one)


def solve_layers(products, noise, layer_count, res_count):
    block_a = products[:, :layer_count, :layer_count]
    block_b = products[:, :layer_count, layer_count : 2 * layer_count]
    block_c = products[:, layer_count : 2 * layer_count, :layer_count]
    block_d = products[:, layer_count : 2 * layer_count, layer_count : 2 * layer_count]
    identity = jnp.eye(layer_count, dtype=jnp.float32)
    gram_real = block_a + block_d + identity[None] * noise[:, :, None]
    gram_imag = block_b - block_c
    system = jnp.concatenate(
        [jnp.concatenate([gram_real, -gram_imag], 2), jnp.concatenate([gram_imag, gram_real], 2)], 1
    )
    matched = products[:, :, 2 * layer_count :]
    match_real = matched[:, :layer_count, :res_count] + matched[:, layer_count:, res_count:]
    match_imag = matched[:, :layer_count, res_count:] - matched[:, layer_count:, :res_count]
    right_side = jnp.concatenate([match_real, match_imag], 1)
    factor = jnp.linalg.cholesky(system)
    solved = jax.vmap(solve_one)(factor, right_side)
    rows = jnp.concatenate([solved[:, :layer_count], solved[:, layer_count:]], 2)
    return rows.reshape(-1, 2 * res_count)


def panel_beams(
    channel_panel,
    signal_panel,
    keep_panel,
    beam_table_real,
    beam_table_imag,
    layer_count,
    res_count,
):
    blocks = NBLK
    block_size = beam_table_real.shape[0] // blocks
    selector = (
        keep_panel[:, :, None] == jnp.arange(blocks, dtype=jnp.int32)[None, None, :]
    ).astype(jnp.bfloat16)

    def apply_all(signal, width):
        first = jnp.einsum(
            "qa,pac->pqc", beam_table_real, signal, preferred_element_type=jnp.float32
        )
        second = jnp.einsum(
            "qa,pac->pqc", beam_table_imag, signal, preferred_element_type=jnp.float32
        )
        return combine_parts(first, second, width)

    beams = jnp.concatenate(
        [apply_all(channel_panel, layer_count), apply_all(signal_panel, res_count)], axis=-1
    )
    shaped = beams.reshape(beams.shape[0], blocks, block_size, beams.shape[-1])
    kept = jnp.einsum(
        "pkb,pbjc->pkjc", selector, shaped, preferred_element_type=jnp.float32
    ).astype(jnp.bfloat16)
    return kept.reshape(beams.shape[0], -1, beams.shape[-1])


def route_rows(rows, owner_rows, devices, capacity):
    highest = lax.Precision.HIGHEST
    total = rows.shape[0]
    onehot = (owner_rows[:, None] == jnp.arange(devices, dtype=jnp.int32)[None, :]).astype(
        jnp.float32
    )
    earlier = (jnp.arange(total)[:, None] > jnp.arange(total)[None, :]).astype(jnp.float32)
    counts = jnp.dot(earlier, onehot, precision=highest)
    slots = jnp.sum(counts * onehot, axis=1)
    place = onehot[:, :, None] * (
        slots[:, None, None] == jnp.arange(capacity).astype(jnp.float32)[None, None, :]
    ).astype(jnp.float32)
    return jnp.einsum("rdk,rc->dkc", place, rows, precision=highest)


def body(channel, received, keep_list, alloc, noise_var, owner):
    beam_table_real, beam_table_imag = beamspace_tables(ANTENNA_EDGE)
    layer_count = channel.shape[-1] // 2
    res_count = received.shape[-1] // 2

    def per_panel(items):
        return panel_beams(
            items[0], items[1], items[2], beam_table_real, beam_table_imag, layer_count, res_count
        )

    kept = lax.map(per_panel, (channel, received, keep_list))
    panel_count = lax.axis_size("panel")
    prb_count = lax.axis_size("prb")
    prb_local = channel.shape[1]
    prb_own = prb_local // panel_count
    products = lax.psum_scatter(
        jnp.einsum(
            "mkqc,mkqd->kcd", kept[..., : 2 * layer_count], kept, preferred_element_type=jnp.float32
        ),
        "panel",
        scatter_dimension=0,
        tiled=True,
    )
    first_prb = lax.axis_index("prb") * prb_local + lax.axis_index("panel") * prb_own
    alloc_rows = lax.dynamic_slice_in_dim(alloc, first_prb, prb_own, 0)
    owner_rows = lax.dynamic_slice_in_dim(owner, first_prb, prb_own, 0).reshape(-1)
    matches = (
        alloc_rows[:, :, None] == jnp.arange(noise_var.shape[0], dtype=jnp.int32)[None, None, :]
    )
    noise = jnp.sum(jnp.where(matches, noise_var[None, None, :], jnp.float32(0.0)), axis=-1)
    layer_rows = solve_layers(products, noise, layer_count, res_count)
    devices = panel_count * prb_count
    capacity = max(2, 2 * prb_own * layer_count // devices)
    outgoing = route_rows(layer_rows, owner_rows, devices, capacity)
    arrived = lax.all_to_all(outgoing, ("panel", "prb"), split_axis=0, concat_axis=0, tiled=True)
    return arrived.reshape(-1, outgoing.shape[-1])


def solution(mesh):
    placed = (
        P("panel", "prb", None, None),
        P("panel", "prb", None, None),
        P("panel", "prb", None),
        P(),
        P(),
        P(),
    )
    return jax.shard_map(
        body, mesh=mesh, in_specs=placed, out_specs=P(("panel", "prb"), None), check_vma=False
    )
```

profile of v0, /device:TPU:0, one launch (start us, length us, event | category | flops | bytes accessed | tf_op | source)
XLA Modules:
  0.0 325.8 jit_solution(9024708489528183299)
XLA Ops:
  6.5 156.2 %while.13 = (s32[]{:T(128)}, bf16[14,16,48,416]{3,2,0,1:T(8,128)(2,1)}, s32[14,16,3]{1,0,2:T(8,128)}, bf16[14,16,64,128]{3,2,1,0:T(8,128)(2,1)}, bf16[14,16,64,2...) while((s32[]{:T(128)}, ...), condition=%wide.region_2.3_spmd.clone.clone.clone, body=%wide.region_1.2_spmd.clone.clone.clone.sunk | while | flops 116490432 | bytes 15672757 | solution.py:117
  6.6 1.7 convolution_bitcast_fusion.8
  8.2 1.7 convolution_bitcast_fusion.9
  19.4 1.7 convolution_bitcast_fusion.9
  30.5 1.7 convolution_bitcast_fusion.9
  40.0 1.7 convolution_bitcast_fusion.8
  41.7 1.7 convolution_bitcast_fusion.9
  52.8 1.7 convolution_bitcast_fusion.9
  62.3 1.7 convolution_bitcast_fusion.8
  64.0 1.7 convolution_bitcast_fusion.9
  75.1 1.7 convolution_bitcast_fusion.9
  86.3 1.7 convolution_bitcast_fusion.9
  97.5 1.7 convolution_bitcast_fusion.9
  107.0 1.7 convolution_bitcast_fusion.8
  108.7 1.7 convolution_bitcast_fusion.9
  119.9 1.7 convolution_bitcast_fusion.9
  131.0 1.7 convolution_bitcast_fusion.9
  140.5 1.7 convolution_bitcast_fusion.8
  151.6 1.7 convolution_bitcast_fusion.8
  162.8 10.3 %fusion.66 = f32[16,128,416]{1,2,0:T(8,128)} fusion(bf16[14,16,48,416]{3,2,0,1:T(8,128)(2,1)} %get-tuple-element.48), kind=kOutput, calls=%fused_computation.77 | convolution fusion | flops 1145044992 | bytes 17170432 | tf_op jit(solution)/shard_map/mkqc,mkqd->kcd/dot_general | solution.py:123
  174.4 78.9 %reduce-scatter.2.cloned.1.call-done = f32[2,128,416]{1,2,0:T(8,128)} async-done(((f32[16,128,416]{1,2,0:T(8,128)}), f32[2,128,416]{1,2,0:T(8,128)}) %reduce-scatter.2.cloned.1.call-update) | async-done | bytes 426000 | tf_op jit(solution)/shard_map/reduce_scatter | solution.py:122
  254.7 23.6 %custom-call.11 = f32[2,128,128]{2,1,0:T(8,128)S(1)} custom-call(f32[2,128,128]{2,1,0:T(8,128)S(1)} %fusion.77), custom_call_target="Cholesky" | custom-call | tf_op jit(solution)/shard_map/jit(cholesky)/cholesky | solution.py:52
  278.6 19.7 %custom-call.12 = f32[2,1,128,128]{2,3,1,0:T(8,128)S(1)} custom-call(f32[2,1,128,128]{3,2,1,0:T(8,128)S(1)} %select_bitcast_fusion), custom_call_target="InvertDiagBlocksLowerTriangular" | custom-call | tf_op jit(solution)/shard_map/vmap(jit(_cho_solve))/triangular_solve | solution.py:34
  301.1 17.0 %all_to_all.5 = f32[32,8,288]{2,1,0:T(8,128)S(1)} all-to-all(f32[32,8,288]{2,1,0:T(8,128)S(1)} %fusion.78), channel_id=1, replica_groups=mesh['panel'=8,'prb'=4] {'panel','prb'}, dimensions={0} | all-to-all | bytes 589824 | tf_op jit(solution)/shard_map/all_to_all | solution.py:141
  (240 shorter events, 131.2 us)
Async XLA Ops:
  6.5 166.6 %copy-start = (s32[64,64,1]{1,2,0:T(1,128)S(1)}, s32[64,64,1]{1,2,0:T(1,128)}, u32[]{:S(2)}) copy-start(s32[64,64,1]{1,2,0:T(1,128)} %param.13) | copy-start | bytes 49156
  6.5 246.8 %reduce-scatter.2.cloned.1.call-start = ((), (), s32[]{:S(2)}) async-start(), calls=%async_computation.2 | async-start | bytes 3833856 | tf_op jit(solution)/shard_map/reduce_scatter | solution.py:122
  162.8 11.4 %copy-start.1 = (f32[512]{0:T(512)S(1)}, f32[512]{0:T(512)}, u32[]{:S(2)}) copy-start(f32[512]{0:T(512)} %param.12) | copy-start | bytes 6148
Sparse Core Ops, SparseCore 0:
  173.2 80.0 reduce-scatter.1
where the time goes:
time: 329 us; the launch traced here: 326 us
  matrix products  114 us (35%)
  waiting for transfers between devices  79 us (24%)
  other arithmetic  60.3 us (18%)
  local copies, waits for them, and re-layouts  40.8 us (12%)
  blocking collectives  17 us (5%)
  between operations  13.5 us (4%)
    reduce_scatter x1, waiting for transfers between devices, body(): lax.psum_scatter(jnp.einsum('mkqc,mkqd->kcd', kept[..., :2 * layer_count]...  78.9 us
    dot_general x28, matrix products, apply_all(): jnp.einsum('qa,pac->pqc', beam_table_imag, signal, preferred_element_type...  42.5 us
    dot_general x28, matrix products, apply_all(): jnp.einsum('qa,pac->pqc', beam_table_real, signal, preferred_element_type...  42.5 us
    another operation x4, other arithmetic, solve_layers(): factor = jnp.linalg.cholesky(system)  23.8 us
    another operation x3, other arithmetic, solve_one(): return jax.scipy.linalg.cho_solve((factor_one, True), right_one)  19.8 us
    dot_general x14, matrix products, panel_beams(): jnp.einsum('pkb,pbjc->pkjc', selector, shaped, preferred_element_type=jnp...  17.3 us
    all_to_all x1, blocking collectives, body(): lax.all_to_all(outgoing, ('panel', 'prb'), split_axis=0, concat_axis=0, t...  17 us
    another operation x28, other arithmetic  13.9 us
  transfers between devices with their start and end apart: 1, of which 1 were waited for; matrix products, arithmetic and copies ran while one was open for 0% of the time, Pallas kernels for 0%

commit v1 on v0

v1 whole, which is shorter than its diff:
```python
import functools
import math

import jax
import jax.numpy as jnp
from jax import lax
from jax.experimental import pallas as pl
from jax.experimental.pallas import tpu as pltpu
from jax.sharding import PartitionSpec as P

ANTENNA_EDGE = 8
NBLK = 4


def beam_matrix(panel_side):
    length = panel_side * panel_side
    positions = jnp.arange(length, dtype=jnp.int32)
    first_axis = positions // panel_side
    second_axis = positions % panel_side
    phases = (
        first_axis[:, None] * first_axis[None, :] + second_axis[:, None] * second_axis[None, :]
    ) % panel_side
    angles = phases.astype(jnp.float32) * (2.0 * math.pi / panel_side)
    real_part = (jnp.cos(angles) / panel_side).astype(jnp.bfloat16)
    imag_part = (-jnp.sin(angles) / panel_side).astype(jnp.bfloat16)
    return jnp.concatenate(
        [
            jnp.concatenate([real_part, -imag_part], 1),
            jnp.concatenate([imag_part, real_part], 1),
        ],
        0,
    )


def products_kernel(layers, res, h_ref, y_ref, mask_ref, f_ref, out_ref, left, right):
    panels = h_ref.shape[0]
    stack = f_ref.shape[0]
    lane = lax.broadcasted_iota(jnp.int32, (layers, stack), 1)
    sign = jnp.where(lane < stack // 2, -1.0, 1.0).astype(jnp.bfloat16)
    for n in range(panels):
        h = h_ref[n, 0]
        y = y_ref[n, 0]
        top = jnp.concatenate([y[:, :res], h[:, :layers]], 1)
        low = jnp.concatenate([y[:, res:], h[:, layers:]], 1)
        stacked = jnp.concatenate([top, low], 0)
        beams = jnp.dot(f_ref[...], stacked, preferred_element_type=jnp.float32).astype(
            jnp.bfloat16
        )
        right[n * stack : (n + 1) * stack, :] = beams
        cut = res // 128 * 128
        turned = beams[:, cut:].T[res - cut :]
        turned = turned * mask_ref[0, :, n * stack : (n + 1) * stack]
        swapped = pltpu.roll(turned.astype(jnp.float32), stack // 2, 1).astype(jnp.bfloat16)
        left[:layers, n * stack : (n + 1) * stack] = turned
        left[layers:, n * stack : (n + 1) * stack] = swapped * sign
    out_ref[0] = jnp.dot(left[...], right[...], preferred_element_type=jnp.float32).astype(
        out_ref.dtype
    )


def solve_kernel(
    layers, res, devices, slots, parts_ref, alloc_ref, noise_ref, owner_ref, out_ref, re, im
):
    sources, own = parts_ref.shape[0], parts_ref.shape[1]
    users = noise_ref.shape[1]
    rows = own * layers
    width = layers + res
    cut = res // 128 * 128
    off = res - cut
    first = lax.axis_index("prb") * (own * lax.axis_size("panel")) + lax.axis_index("panel") * own
    highest = lax.Precision.HIGHEST

    row_id = lax.broadcasted_iota(jnp.int32, (layers, 128), 0)
    lane_id = lax.broadcasted_iota(jnp.int32, (layers, 128), 1)
    owners = []
    for p in range(own):
        total = parts_ref[0, p].astype(jnp.float32)
        for s in range(1, sources):
            total = total + parts_ref[s, p].astype(jnp.float32)
        named = alloc_ref[pl.ds(first + p, 1), :]
        picks = (
            lax.broadcasted_iota(jnp.int32, (users, layers), 0) == named
        ).astype(jnp.float32)
        noise = jnp.dot(noise_ref[...], picks, precision=highest)
        spread = jnp.concatenate(
            [jnp.zeros((1, off), jnp.float32), noise, jnp.zeros((1, 128 - off - layers), jnp.float32)],
            1,
        )
        re[p, :, :cut] = total[:layers, :cut]
        im[p, :, :cut] = total[layers:, :cut]
        filler = jnp.zeros((layers, cut + 128 - width), jnp.float32)
        re[p, :, cut:] = jnp.concatenate([total[:layers, cut:], filler], 1) + jnp.where(
            row_id + off == lane_id, spread, 0.0
        )
        im[p, :, cut:] = jnp.concatenate([total[layers:, cut:], filler], 1)
        owners.append(owner_ref[pl.ds(first + p, 1), :])

    def step(k, carry):
        at = jnp.full((layers, 128), 0, jnp.int32) + (k + off)
        for p in range(own):
            a = re[p]
            b = im[p]
            col_r = jnp.take_along_axis(a[:, cut:], at, axis=1)
            col_i = jnp.take_along_axis(b[:, cut:], at, axis=1)
            row_r = re[p, pl.ds(k, 1), :]
            row_i = im[p, pl.ds(k, 1), :]
            tail = jnp.broadcast_to(row_r[:, cut:], (8, 128))
            pivot = jnp.take_along_axis(tail, at[:8], axis=1)
            inverse = 1.0 / pivot[:1]
            inverse = jnp.concatenate([inverse] * (cut // 128 + 1), 1)
            row_r = row_r * inverse
            row_i = row_i * inverse
            col_r = jnp.concatenate([col_r] * (cut // 128 + 1), 1)
            col_i = jnp.concatenate([col_i] * (cut // 128 + 1), 1)
            re[p] = a - (col_r * row_r - col_i * row_i)
            im[p] = b - (col_r * row_i + col_i * row_r)
            re[p, pl.ds(k, 1), :] = row_r
            im[p, pl.ds(k, 1), :] = row_i
        return carry

    lax.fori_loop(0, layers, step, 0)

    owner = jnp.concatenate(owners, 1)
    who = (lax.broadcasted_iota(jnp.int32, (devices, rows), 0) == owner).astype(jnp.float32)
    earlier = (
        lax.broadcasted_iota(jnp.int32, (rows, rows), 0)
        < lax.broadcasted_iota(jnp.int32, (rows, rows), 1)
    ).astype(jnp.bfloat16)
    counts = jnp.dot(who.astype(jnp.bfloat16), earlier, preferred_element_type=jnp.float32)
    slot = jnp.sum(counts * who, axis=0, keepdims=True).astype(jnp.int32)
    target = owner * slots + slot
    place = (
        lax.broadcasted_iota(jnp.int32, (devices * slots, rows), 0) == target
    ).astype(jnp.bfloat16)
    real = jnp.concatenate([re[p, :, :res] for p in range(own)], 0).astype(jnp.bfloat16)
    imag = jnp.concatenate([im[p, :, :res] for p in range(own)], 0).astype(jnp.bfloat16)
    real = jnp.dot(place, real, preferred_element_type=jnp.float32)
    imag = jnp.dot(place, imag, preferred_element_type=jnp.float32)
    out_ref[...] = jnp.concatenate(
        [real.reshape(devices, slots, res), imag.reshape(devices, slots, res)], 1
    ).astype(jnp.bfloat16)


def body(channel, received, keep_list, alloc, noise_var, owner):
    table = beam_matrix(ANTENNA_EDGE)
    layers = channel.shape[-1] // 2
    res = received.shape[-1] // 2
    panels, prb_local, antennas = channel.shape[:3]
    panel_count = lax.axis_size("panel")
    devices = panel_count * lax.axis_size("prb")
    own = prb_local // panel_count
    capacity = max(2, 2 * own * layers // devices)
    slots = -(-capacity // 8) * 8
    stack = 2 * antennas
    width = layers + res

    blocks = jnp.arange(antennas, dtype=jnp.int32) // (antennas // NBLK)
    mask = jnp.any(keep_list[:, :, :, None] == blocks[None, None, None, :], axis=2)
    mask = jnp.concatenate([mask, mask], -1).astype(jnp.bfloat16)
    mask = jnp.transpose(mask, (1, 0, 2)).reshape(prb_local, 1, panels * stack)

    products = pl.pallas_call(
        functools.partial(products_kernel, layers, res),
        out_shape=jax.ShapeDtypeStruct((prb_local, 2 * layers, width), jnp.bfloat16),
        grid=(prb_local,),
        in_specs=[
            pl.BlockSpec((panels, 1, antennas, 2 * layers), lambda p: (0, p, 0, 0)),
            pl.BlockSpec((panels, 1, antennas, 2 * res), lambda p: (0, p, 0, 0)),
            pl.BlockSpec((1, 1, panels * stack), lambda p: (p, 0, 0)),
            pl.BlockSpec((stack, stack), lambda p: (0, 0)),
        ],
        out_specs=pl.BlockSpec((1, 2 * layers, width), lambda p: (p, 0, 0)),
        scratch_shapes=[
            pltpu.VMEM((2 * layers, panels * stack), jnp.bfloat16),
            pltpu.VMEM((panels * stack, width), jnp.bfloat16),
        ],
        compiler_params=pltpu.CompilerParams(vmem_limit_bytes=48 << 20),
    )(channel, received, mask, table)

    parts = lax.all_to_all(
        products.reshape(panel_count, own, 2 * layers, width), "panel", 0, 0, tiled=True
    )
    outgoing = pl.pallas_call(
        functools.partial(solve_kernel, layers, res, devices, slots),
        out_shape=jax.ShapeDtypeStruct((devices, 2 * slots, res), jnp.bfloat16),
        in_specs=[pl.BlockSpec(memory_space=pltpu.VMEM)] * 4,
        out_specs=pl.BlockSpec(memory_space=pltpu.VMEM),
        scratch_shapes=[
            pltpu.VMEM((own, layers, res // 128 * 128 + 128), jnp.float32),
            pltpu.VMEM((own, layers, res // 128 * 128 + 128), jnp.float32),
        ],
        compiler_params=pltpu.CompilerParams(vmem_limit_bytes=48 << 20),
    )(parts, alloc, noise_var.reshape(1, -1), owner.reshape(alloc.shape))
    arrived = lax.all_to_all(outgoing, ("panel", "prb"), split_axis=0, concat_axis=0, tiled=True)
    rows = jnp.concatenate(
        [arrived[:, :capacity], arrived[:, slots : slots + capacity]], -1
    ).astype(jnp.float32)
    return rows.reshape(-1, 2 * res)


def solution(mesh):
    placed = (
        P("panel", "prb", None, None),
        P("panel", "prb", None, None),
        P("panel", "prb", None),
        P(),
        P(),
        P(),
    )
    return jax.shard_map(
        body, mesh=mesh, in_specs=placed, out_specs=P(("panel", "prb"), None), check_vma=False
    )
```

time: 329 us -> 81.5 us (0.25)
  matrix products: 114 us -> 0 us
  waiting for transfers between devices: 79 us -> 0 us
  other arithmetic: 60.3 us -> 1.52 us
  local copies, waits for them, and re-layouts: 40.8 us -> 4.21 us
  Pallas kernels: 0 us -> 32.4 us
  blocking collectives: 17 us -> 42.7 us
  between operations: 13.5 us -> 0.13 us
    dot_general x73 -> x0, matrix products: 113 us -> none  [the longest x28 42.5 us: apply_all(): jnp.einsum('qa,pac->pqc', beam_table_imag, signal, preferred_element_type...]
    reduce_scatter x1 -> x0, waiting for transfers between devices: 78.9 us -> none  [body(): lax.psum_scatter(jnp.einsum('mkqc,mkqd->kcd', kept[..., :2 * layer_count]...]
    another operation x35 -> x0, other arithmetic: 57.5 us -> none  [the longest x4 23.8 us: solve_layers(): factor = jnp.linalg.cholesky(system)]
    pallas_call x0 -> x2, Pallas kernels: none -> 32.4 us  [the longest x1 18.1 us: body(): pl.pallas_call(functools.partial(products_kernel, layers, res), out_shape...]
    all_to_all x0 -> x1, blocking collectives: none -> 29.3 us  [body(): lax.all_to_all(products.reshape(panel_count, own, 2 * layers, width), 'pa...]
    dynamic_update_slice x14 -> x0, local copies, waits for them, and re-layouts: 13.6 us -> none  [body(): kept = lax.map(per_panel, (channel, received, keep_list))]
    concatenate x58 -> x3, local copies, waits for them, and re-layouts: 11.1 us -> 0.22 us  [body(): jnp.concatenate([arrived[:, :capacity], arrived[:, slots:slots + capacity...]
    dynamic_slice x30 -> x0, local copies, waits for them, and re-layouts: 10.9 us -> none  [the longest x28 10.1 us: body(): kept = lax.map(per_panel, (channel, received, keep_list))]
  transfers between devices with their start and end apart: 1 -> 0, of which waited for: 1 -> 0; matrix products, arithmetic and copies ran while one was open for 0% -> 0% of each run, Pallas kernels for 0% -> 0%
where the time goes in v1:
time: 81.5 us; the launch traced here: 80.9 us
  blocking collectives  42.7 us (52%)
  Pallas kernels  32.4 us (40%)
  local copies, waits for them, and re-layouts  4.21 us (5%)
  other arithmetic  1.52 us (2%)
    all_to_all x1, blocking collectives, body(): lax.all_to_all(products.reshape(panel_count, own, 2 * layers, width), 'pa...  29.3 us
    pallas_call x1, Pallas kernels, body(): pl.pallas_call(functools.partial(products_kernel, layers, res), out_shape...  18.1 us
    pallas_call x1, Pallas kernels, body(): pl.pallas_call(functools.partial(solve_kernel, layers, res, devices, slot...  14.3 us
    all_to_all x1, blocking collectives, body(): lax.all_to_all(outgoing, ('panel', 'prb'), split_axis=0, concat_axis=0, t...  13.4 us
    unnamed x9, local copies, waits for them, and re-layouts  2.8 us

profile of v1, /device:TPU:0, one launch (start us, length us, event | category | flops | bytes accessed | tf_op | source)
XLA Modules:
  0.0 80.9 jit_solution(8122396994385422275)
XLA Ops:
  0.0 0.0 copy-start.1
  0.0 0.0 copy-start.2
  0.0 0.0 copy-start.3
  0.0 0.2 fusion.4
  0.2 0.2 multiply_convert_fusion
  0.5 0.8 copy.20
  1.2 0.2 compare_reduce_fusion
  1.4 0.1 fusion
  1.6 0.1 maximum_maximum_fusion.f_ref
  1.6 0.0 copy-start
  1.7 2.0 %copy-done = bf16[14,16,64,128]{3,2,1,0:T(8,128)(2,1)S(1)} copy-done((bf16[14,16,64,128]{3,2,1,0:T(8,128)(2,1)S(1)}, bf16[14,16,64,128]{3,2,1,0:T(8,128)(2,1)}, u32[]{:S(2)}) %copy-start) | copy-done | bytes 3670040
  3.7 18.1 %shard_map.64 = bf16[16,128,208]{2,1,0:T(8,128)(2,1)S(1)} custom-call(bf16[14,16,64,128]{3,2,1,0:T(8,128)(2,1)S(1)} %copy-done, bf16[14,16,64,288]{3,2,1,0:T(8,128)(2,1)} %y_ref.1, bf16[16,1,1792]{2,1,0:T(2,128)(2,1)S(1)} %reshape.87.mask_ref, bf16[128,128]{1,0:T(8,128)(2,1)S(1)} %maximum_maximum_fusion.f_ref), custom_call_target="tpu_custom_call" | custom-call | tf_op jit(solution)/shard_map/pallas_call | solution.py:162
  21.8 0.6 copy.23
  22.5 29.3 %all_to_all.10 = bf16[8,2,128,208]{2,3,1,0:T(8,128)(2,1)S(1)} all-to-all(bf16[8,2,128,208]{2,3,1,0:T(8,128)(2,1)S(1)} %copy.23), channel_id=1, replica_groups=mesh['panel'=8,'prb'=4] {'panel'}, dimensions={0} | all-to-all | bytes 1703936 | tf_op jit(solution)/shard_map/all_to_all | solution.py:180
  51.7 0.5 copy.24.parts_ref
  52.2 0.0 copy-done.1
  52.2 0.0 copy-done.2
  52.2 0.0 copy-done.3
  52.3 14.3 %shard_map.65 = bf16[32,16,144]{2,1,0:T(8,128)(2,1)S(1)} custom-call(bf16[8,2,128,208]{3,2,1,0:T(8,128)(2,1)S(1)} %copy.24.parts_ref, s32[64,64]{1,0:T(8,128)S(1)} %copy-done.1, f32[1,512]{1,0:T(1,128)S(1)} %bitcast.11, s32[64,64]{1,0:T(8,128)S(1)} %bitcast.10), custom_call_target="tpu_custom_call" | custom-call | tf_op jit(solution)/shard_map/pallas_call | solution.py:183
  66.5 13.4 %all_to_all.11 = bf16[32,16,144]{2,1,0:T(8,128)(2,1)S(1)} all-to-all(bf16[32,16,144]{2,1,0:T(8,128)(2,1)S(1)} %shard_map.65), channel_id=1, replica_groups=mesh['panel'=8,'prb'=4] {'panel','prb'}, dimensions={0} | all-to-all | bytes 294912 | tf_op jit(solution)/shard_map/all_to_all | solution.py:194
  80.0 0.1 copy.25
  80.1 0.1 copy.26
  80.2 0.7 maximum_convert_fusion
  (5 shorter events, 0.1 us)
Async XLA Ops:
  0.0 52.2 %copy-start.1 = (s32[64,64]{1,0:T(8,128)S(1)}, s32[64,64]{1,0:T(8,128)}, u32[]{:S(2)}) copy-start(s32[64,64]{1,0:T(8,128)} %alloc_ref.1) | copy-start | bytes 49156
  0.0 52.2 %copy-start.2 = (s32[64,64,1]{1,2,0:T(1,128)S(1)}, s32[64,64,1]{1,2,0:T(1,128)}, u32[]{:S(2)}) copy-start(s32[64,64,1]{1,2,0:T(1,128)} %param.11) | copy-start | bytes 49156
  0.0 52.2 %copy-start.3 = (f32[512]{0:T(512)S(1)}, f32[512]{0:T(512)}, u32[]{:S(2)}) copy-start(f32[512]{0:T(512)} %param.10) | copy-start | bytes 6148
  1.6 2.0 %copy-start = (bf16[14,16,64,128]{3,2,1,0:T(8,128)(2,1)S(1)}, bf16[14,16,64,128]{3,2,1,0:T(8,128)(2,1)}, u32[]{:S(2)}) copy-start(bf16[14,16,64,128]{3,2,1,0:T(8,128)(2,1)} %h_ref.1) | copy-start | bytes 11010052

commit v2 on v1

v2 whole, which is shorter than its diff:
```python
import functools
import math

import jax
import jax.numpy as jnp
import numpy as np
from jax import lax
from jax.experimental import pallas as pl
from jax.experimental.pallas import tpu as pltpu
from jax.sharding import PartitionSpec as P

ANTENNA_EDGE = 8
NBLK = 4


def beam_matrix(panel_side):
    positions = np.arange(panel_side * panel_side)
    first_axis = positions // panel_side
    second_axis = positions % panel_side
    phases = (
        first_axis[:, None] * first_axis[None, :] + second_axis[:, None] * second_axis[None, :]
    ) % panel_side
    angles = phases.astype(np.float32) * np.float32(2.0 * math.pi / panel_side)
    real_part = np.cos(angles) / panel_side
    imag_part = -np.sin(angles) / panel_side
    return np.concatenate(
        [
            np.concatenate([real_part, -imag_part], 1),
            np.concatenate([imag_part, real_part], 1),
        ],
        0,
    ).astype(jnp.bfloat16)


def products_kernel(
    layers,
    res,
    own,
    h_ref,
    y_ref,
    keep_ref,
    f_ref,
    out_ref,
    left,
    right,
    masks,
    sent,
    held,
    send_sem,
    recv_sem,
):
    panels = h_ref.shape[0]
    stack = f_ref.shape[0]
    antennas = stack // 2
    kmax = keep_ref.shape[0]
    peers = lax.axis_size("panel")
    me = lax.axis_index("panel")
    turn = pl.program_id(0)
    offset = turn // own + 1
    peer = lax.rem(me + offset, peers)
    part = lax.rem(turn, own)
    barrier = pltpu.get_barrier_semaphore()

    def copy(there, slot, j):
        return pltpu.make_async_remote_copy(
            src_ref=sent.at[there, j],
            dst_ref=held.at[slot, j],
            send_sem=send_sem.at[there, j],
            recv_sem=recv_sem.at[slot, j],
            device_id={"panel": there},
            device_id_type=pl.DeviceIdType.MESH,
        )

    @pl.when(turn == 0)
    def _():
        for step in range(1, peers):
            pl.semaphore_signal(
                barrier,
                inc=1,
                device_id={"panel": lax.rem(me + step, peers)},
                device_id_type=pl.DeviceIdType.MESH,
            )
        block = (
            lax.rem(lax.broadcasted_iota(jnp.int32, (1, stack), 1), antennas)
            // (antennas // NBLK)
        ).astype(jnp.float32)
        names = [keep_ref[k].astype(jnp.float32).T for k in range(kmax)]
        for n in range(panels):
            hit = names[0][:, n : n + 1] == block
            for k in range(1, kmax):
                hit = hit | (names[k][:, n : n + 1] == block)
            masks[:, n * stack : (n + 1) * stack] = jnp.where(hit, 1.0, 0.0)

    lane = lax.broadcasted_iota(jnp.int32, (layers, stack), 1)
    sign = jnp.where(lane < antennas, -1.0, 1.0)
    mask = masks[pl.ds(peer * own + part, 1), :]
    for n in range(panels):
        h = h_ref[n, 0]
        y = y_ref[n, 0]
        top = jnp.concatenate([y[:, :res], h[:, :layers]], 1)
        low = jnp.concatenate([y[:, res:], h[:, layers:]], 1)
        stacked = jnp.concatenate([top, low], 0)
        beams = jnp.dot(f_ref[...], stacked, preferred_element_type=jnp.float32).astype(
            jnp.bfloat16
        )
        right[n * stack : (n + 1) * stack, :] = beams
        cut = res // 128 * 128
        turned = beams[:, cut:].T[res - cut :].astype(jnp.float32)
        turned = turned * mask[:, n * stack : (n + 1) * stack]
        swapped = pltpu.roll(turned, antennas, 1) * sign
        left[:layers, n * stack : (n + 1) * stack] = turned.astype(jnp.bfloat16)
        left[layers:, n * stack : (n + 1) * stack] = swapped.astype(jnp.bfloat16)
    sent[peer, part] = jnp.dot(
        left[...], right[...], preferred_element_type=jnp.float32
    ).astype(sent.dtype)

    @pl.when(turn == 0)
    def _():
        pl.semaphore_wait(barrier, peers - 1)

    @pl.when(offset < peers)
    def _():
        copy(peer, me, part).start()

    @pl.when(turn == pl.num_programs(0) - 1)
    def _():
        for j in range(own):
            total = sent[me, j].astype(jnp.float32)
            for step in range(1, peers):
                source = lax.rem(me + peers - step, peers)
                copy(source, source, j).wait_recv()
                total = total + held[source, j].astype(jnp.float32)
            out_ref[j] = total
        for j in range(own):
            for step in range(1, peers):
                there = lax.rem(me + step, peers)
                copy(there, me, j).wait_send()


def solve_kernel(
    layers,
    res,
    capacity,
    slots,
    parts_ref,
    alloc_ref,
    noise_ref,
    owner_ref,
    out_ref,
    re,
    im,
    sent,
    held,
    send_sem,
    recv_sem,
):
    own = parts_ref.shape[0]
    users = noise_ref.shape[1]
    rows = own * layers
    width = layers + res
    cut = res // 128 * 128
    off = res - cut
    prbs = lax.axis_size("prb")
    devices = lax.axis_size("panel") * prbs
    me = lax.axis_index("panel") * prbs + lax.axis_index("prb")
    first = lax.axis_index("prb") * (own * lax.axis_size("panel")) + lax.axis_index("panel") * own
    highest = lax.Precision.HIGHEST
    barrier = pltpu.get_barrier_semaphore()

    def at_device(there):
        return {"panel": there // prbs, "prb": lax.rem(there, prbs)}

    def copy(there, slot):
        return pltpu.make_async_remote_copy(
            src_ref=sent.at[there],
            dst_ref=held.at[slot],
            send_sem=send_sem.at[there],
            recv_sem=recv_sem.at[slot],
            device_id=at_device(there),
            device_id_type=pl.DeviceIdType.MESH,
        )

    def greet(step, carry):
        pl.semaphore_signal(
            barrier,
            inc=1,
            device_id=at_device(lax.rem(me + step, devices)),
            device_id_type=pl.DeviceIdType.MESH,
        )
        return carry

    lax.fori_loop(1, devices, greet, 0)

    row_id = lax.broadcasted_iota(jnp.int32, (layers, 128), 0)
    lane_id = lax.broadcasted_iota(jnp.int32, (layers, 128), 1)
    owners = []
    for p in range(own):
        total = parts_ref[p]
        named = alloc_ref[pl.ds(first + p, 1), :]
        picks = (
            lax.broadcasted_iota(jnp.int32, (users, layers), 0) == named
        ).astype(jnp.float32)
        noise = jnp.dot(noise_ref[...], picks, precision=highest)
        spread = jnp.concatenate(
            [
                jnp.zeros((1, off), jnp.float32),
                noise,
                jnp.zeros((1, 128 - off - layers), jnp.float32),
            ],
            1,
        )
        re[p, :, :cut] = total[:layers, :cut]
        im[p, :, :cut] = total[layers:, :cut]
        filler = jnp.zeros((layers, cut + 128 - width), jnp.float32)
        re[p, :, cut:] = jnp.concatenate([total[:layers, cut:], filler], 1) + jnp.where(
            row_id + off == lane_id, spread, 0.0
        )
        im[p, :, cut:] = jnp.concatenate([total[layers:, cut:], filler], 1)
        owners.append(owner_ref[pl.ds(first + p, 1), :])

    def wide(x):
        return jnp.concatenate([x] * (cut // 128 + 1), 1)

    def step(half, carry):
        k = half * 2
        at = jnp.zeros((layers, 128), jnp.int32) + (k + off)
        at_next = at + 1

        def pick(x, index):
            return jnp.take_along_axis(x, index, axis=1)

        def pick_row(x, index):
            return pick(jnp.broadcast_to(x[:, cut:], (8, 128)), index[:8])[:1]

        results = []
        for p in range(own):
            a, b = re[p], im[p]
            ar, ai = re[p, pl.ds(k, 1), :], im[p, pl.ds(k, 1), :]
            br, bi = re[p, pl.ds(k + 1, 1), :], im[p, pl.ds(k + 1, 1), :]
            first_pivot = pick_row(ar, at)
            cross_r, cross_i = pick_row(ar, at_next), pick_row(ai, at_next)
            second_pivot = pick_row(br, at_next)
            scale = 1.0 / (
                first_pivot * second_pivot - (cross_r * cross_r + cross_i * cross_i)
            )
            f, g = wide(second_pivot * scale), wide(first_pivot * scale)
            cr, ci = wide(cross_r * scale), wide(cross_i * scale)
            ur = f * ar - (cr * br - ci * bi)
            ui = f * ai - (cr * bi + ci * br)
            vr = g * br - (cr * ar + ci * ai)
            vi = g * bi - (cr * ai - ci * ar)
            c1r, c1i = wide(pick(a[:, cut:], at)), wide(pick(b[:, cut:], at))
            c2r, c2i = wide(pick(a[:, cut:], at_next)), wide(pick(b[:, cut:], at_next))
            na = a - ((c1r * ur - c1i * ui) + (c2r * vr - c2i * vi))
            nb = b - ((c1r * ui + c1i * ur) + (c2r * vi + c2i * vr))
            results.append((na, nb, ur, ui, vr, vi))
        for p in range(own):
            na, nb, ur, ui, vr, vi = results[p]
            re[p] = na
            im[p] = nb
            re[p, pl.ds(k, 1), :] = ur
            im[p, pl.ds(k, 1), :] = ui
            re[p, pl.ds(k + 1, 1), :] = vr
            im[p, pl.ds(k + 1, 1), :] = vi
        return carry

    lax.fori_loop(0, layers // 2, step, 0)

    owner = jnp.concatenate(owners, 1)
    who = (lax.broadcasted_iota(jnp.int32, (devices, rows), 0) == owner).astype(jnp.float32)
    earlier = (
        lax.broadcasted_iota(jnp.int32, (rows, rows), 0)
        < lax.broadcasted_iota(jnp.int32, (rows, rows), 1)
    ).astype(jnp.bfloat16)
    counts = jnp.dot(who.astype(jnp.bfloat16), earlier, preferred_element_type=jnp.float32)
    slot = jnp.sum(counts * who, axis=0, keepdims=True)
    target = owner.astype(jnp.float32) * slots + slot
    place = (
        lax.broadcasted_iota(jnp.int32, (devices * slots, rows), 0).astype(jnp.float32) == target
    ).astype(jnp.bfloat16)
    real = jnp.concatenate([re[p, :, :res] for p in range(own)], 0).astype(jnp.bfloat16)
    imag = jnp.concatenate([im[p, :, :res] for p in range(own)], 0).astype(jnp.bfloat16)
    real = jnp.dot(place, real, preferred_element_type=jnp.float32)
    imag = jnp.dot(place, imag, preferred_element_type=jnp.float32)
    sent[...] = jnp.concatenate(
        [real.reshape(devices, slots, res), imag.reshape(devices, slots, res)], 1
    ).astype(jnp.bfloat16)

    pl.semaphore_wait(barrier, devices - 1)

    def send(step, carry):
        copy(lax.rem(me + step, devices), me).start()
        return carry

    def arrive(step, carry):
        source = lax.rem(me + devices - step, devices)
        copy(source, source).wait_recv()
        return carry

    def leave(step, carry):
        copy(lax.rem(me + step, devices), me).wait_send()
        return carry

    lax.fori_loop(1, devices, send, 0)
    held[me] = sent[me]
    lax.fori_loop(1, devices, arrive, 0)
    rows_in = held[...].astype(jnp.float32)
    out_ref[:, :res] = rows_in[:, :capacity].reshape(devices * capacity, res)
    out_ref[:, res:] = rows_in[:, slots : slots + capacity].reshape(devices * capacity, res)
    lax.fori_loop(1, devices, leave, 0)


def body(channel, received, keep_list, alloc, noise_var, owner):
    table = jnp.asarray(beam_matrix(ANTENNA_EDGE))
    layers = channel.shape[-1] // 2
    res = received.shape[-1] // 2
    panels, prb_local, antennas = channel.shape[:3]
    peers = lax.axis_size("panel")
    devices = peers * lax.axis_size("prb")
    own = prb_local // peers
    capacity = max(2, 2 * own * layers // devices)
    slots = -(-capacity // 8) * 8
    stack = 2 * antennas
    width = layers + res
    kmax = keep_list.shape[-1]

    def prb_of(turn):
        peer = lax.rem(lax.axis_index("panel") + turn // own + 1, peers)
        return peer * own + lax.rem(turn, own)

    totals = pl.pallas_call(
        functools.partial(products_kernel, layers, res, own),
        out_shape=jax.ShapeDtypeStruct((own, 2 * layers, width), jnp.float32),
        grid=(prb_local,),
        in_specs=[
            pl.BlockSpec((panels, 1, antennas, 2 * layers), lambda t: (0, prb_of(t), 0, 0)),
            pl.BlockSpec((panels, 1, antennas, 2 * res), lambda t: (0, prb_of(t), 0, 0)),
            pl.BlockSpec((kmax, panels, prb_local), lambda t: (0, 0, 0)),
            pl.BlockSpec((stack, stack), lambda t: (0, 0)),
        ],
        out_specs=pl.BlockSpec((own, 2 * layers, width), lambda t: (0, 0, 0)),
        scratch_shapes=[
            pltpu.VMEM((2 * layers, panels * stack), jnp.bfloat16),
            pltpu.VMEM((panels * stack, width), jnp.bfloat16),
            pltpu.VMEM((prb_local, panels * stack), jnp.float32),
            pltpu.VMEM((peers, own, 2 * layers, width), jnp.bfloat16),
            pltpu.VMEM((peers, own, 2 * layers, width), jnp.bfloat16),
            pltpu.SemaphoreType.DMA((peers, own)),
            pltpu.SemaphoreType.DMA((peers, own)),
        ],
        compiler_params=pltpu.CompilerParams(
            vmem_limit_bytes=48 << 20, collective_id=0, has_side_effects=True
        ),
    )(channel, received, jnp.transpose(keep_list, (2, 0, 1)), table)

    return pl.pallas_call(
        functools.partial(solve_kernel, layers, res, capacity, slots),
        out_shape=jax.ShapeDtypeStruct((devices * capacity, 2 * res), jnp.float32),
        in_specs=[pl.BlockSpec(memory_space=pltpu.VMEM)] * 4,
        out_specs=pl.BlockSpec(memory_space=pltpu.VMEM),
        scratch_shapes=[
            pltpu.VMEM((own, layers, res // 128 * 128 + 128), jnp.float32),
            pltpu.VMEM((own, layers, res // 128 * 128 + 128), jnp.float32),
            pltpu.VMEM((devices, 2 * slots, res), jnp.bfloat16),
            pltpu.VMEM((devices, 2 * slots, res), jnp.bfloat16),
            pltpu.SemaphoreType.DMA((devices,)),
            pltpu.SemaphoreType.DMA((devices,)),
        ],
        compiler_params=pltpu.CompilerParams(
            vmem_limit_bytes=48 << 20, collective_id=1, has_side_effects=True
        ),
    )(totals, alloc, noise_var.reshape(1, -1), owner.reshape(alloc.shape))


def solution(mesh):
    placed = (
        P("panel", "prb", None, None),
        P("panel", "prb", None, None),
        P("panel", "prb", None),
        P(),
        P(),
        P(),
    )
    return jax.shard_map(
        body, mesh=mesh, in_specs=placed, out_specs=P(("panel", "prb"), None), check_vma=False
    )
```

time: 81.5 us -> 54.1 us (0.66)
  blocking collectives: 42.7 us -> 0 us
  Pallas kernels: 32.4 us -> 49.1 us
  other arithmetic: 1.52 us -> 0 us
    all_to_all x2 -> x0, blocking collectives: 42.7 us -> none  [the longest x1 29.3 us: body(): lax.all_to_all(products.reshape(panel_count, own, 2 * layers, width), 'pa...]
    pallas_call x2, Pallas kernels: 32.4 us -> 49.1 us  [the longest x1 28.8 us: body(): pl.pallas_call(functools.partial(products_kernel, layers, res, own), out_...]
    convert_element_type x2 -> x0, other arithmetic: 0.96 us -> none  [the longest x1 0.74 us: body(): rows = jnp.concatenate([arrived[:, :capacity], arrived[:, slots:slots + c...]
    pallas_call x0 -> x1, local copies, waits for them, and re-layouts: none -> 0.86 us  [body(): pl.pallas_call(functools.partial(solve_kernel, layers, res, capacity, slo...]
    unnamed x9 -> x12, local copies, waits for them, and re-layouts: 2.8 us -> 3.56 us
where the time goes in v2:
time: 54.1 us; the launch traced here: 53.5 us
  Pallas kernels  49.1 us (91%)
  local copies, waits for them, and re-layouts  4.41 us (8%)
    pallas_call x1, Pallas kernels, body(): pl.pallas_call(functools.partial(products_kernel, layers, res, own), out_...  28.8 us
    pallas_call x1, Pallas kernels, body(): pl.pallas_call(functools.partial(solve_kernel, layers, res, capacity, slo...  20.3 us
    unnamed x12, local copies, waits for them, and re-layouts  3.56 us

profile of v2, /device:TPU:0, one launch (start us, length us, event | category | flops | bytes accessed | tf_op | source)
XLA Modules:
  0.0 53.5 jit_solution(8941602726199677391)
XLA Ops:
  0.0 0.0 copy-start.5
  0.0 0.0 copy-start
  0.0 2.0 %copy-done = bf16[14,16,64,128]{3,2,1,0:T(8,128)(2,1)S(1)} copy-done((bf16[14,16,64,128]{3,2,1,0:T(8,128)(2,1)S(1)}, bf16[14,16,64,128]{3,2,1,0:T(8,128)(2,1)}, u32[]{:S(2)}) %copy-start) | copy-done | bytes 3670040
  2.1 0.0 copy-start.1
  2.1 0.8 %copy-done.1 = bf16[128,128]{1,0:T(8,128)(2,1)S(1)} copy-done((bf16[128,128]{1,0:T(8,128)(2,1)S(1)}, bf16[128,128]{1,0:T(8,128)(2,1)}, u32[]{:S(2)}) %copy-start.1) | copy-done | bytes 32792
  2.8 0.0 copy-start.4
  2.8 0.7 %copy-done.4 = s32[14,16,3]{1,0,2:T(8,128)S(1)} copy-done((s32[14,16,3]{1,0,2:T(8,128)S(1)}, s32[14,16,3]{1,0,2:T(8,128)}, u32[]{:S(2)}) %copy-start.4) | copy-done | bytes 2712
  3.6 0.0 copy-start.2
  3.6 0.0 copy-start.3
  3.6 28.8 %shard_map.73.parts_ref = f32[2,128,208]{2,1,0:T(8,128)S(1)} custom-call(bf16[14,16,64,128]{3,2,1,0:T(8,128)(2,1)S(1)} %copy-done, bf16[14,16,64,288]{3,2,1,0:T(8,128)(2,1)} %y_ref.1, s32[3,14,16]{2,1,0:T(8,128)S(1)} %bitcast.4, bf16[128,128]{1,0:T(8,128)(2,1)S(1)} %copy-done.1), custom_call_target="tpu_custom_call" | custom-call | tf_op jit(solution)/shard_map/pallas_call | solution.py:331
  32.3 0.0 copy-done.5
  32.3 0.0 copy-done.2
  32.3 0.0 copy-done.3
  32.4 20.3 %shard_map.74 = f32[256,288]{1,0:T(8,128)S(1)} custom-call(f32[2,128,208]{2,1,0:T(8,128)S(1)} %shard_map.73.parts_ref, s32[64,64]{1,0:T(8,128)S(1)} %copy-done.2, f32[1,512]{1,0:T(1,128)S(1)} %bitcast.5, s32[64,64]{1,0:T(8,128)S(1)} %bitcast.3), custom_call_target="tpu_custom_call" | custom-call | tf_op jit(solution)/shard_map/pallas_call | solution.py:356
  52.7 0.9 %copy.8 = f32[256,288]{0,1:T(8,128)} copy(f32[256,288]{1,0:T(8,128)S(1)} %shard_map.74) | data formatting | bytes 589824 | tf_op jit(solution)/shard_map/pallas_call | solution.py:356
Async XLA Ops:
  0.0 32.3 %copy-start.5 = (f32[512]{0:T(512)S(1)}, f32[512]{0:T(512)}, u32[]{:S(2)}) copy-start(f32[512]{0:T(512)} %param.11) | copy-start | bytes 6148
  0.0 2.1 %copy-start = (bf16[14,16,64,128]{3,2,1,0:T(8,128)(2,1)S(1)}, bf16[14,16,64,128]{3,2,1,0:T(8,128)(2,1)}, u32[]{:S(2)}) copy-start(bf16[14,16,64,128]{3,2,1,0:T(8,128)(2,1)} %h_ref.1) | copy-start | bytes 11010052
  2.1 0.8 %copy-start.1 = (bf16[128,128]{1,0:T(8,128)(2,1)S(1)}, bf16[128,128]{1,0:T(8,128)(2,1)}, u32[]{:S(2)}) copy-start(bf16[128,128]{1,0:T(8,128)(2,1)} %constant.2.clone.f_ref) | copy-start | bytes 98308
  2.8 0.7 %copy-start.4 = (s32[14,16,3]{1,0,2:T(8,128)S(1)}, s32[14,16,3]{1,0,2:T(8,128)}, u32[]{:S(2)}) copy-start(s32[14,16,3]{1,0,2:T(8,128)} %param.9) | copy-start | bytes 8068
  3.6 28.8 %copy-start.2 = (s32[64,64]{1,0:T(8,128)S(1)}, s32[64,64]{1,0:T(8,128)}, u32[]{:S(2)}) copy-start(s32[64,64]{1,0:T(8,128)} %alloc_ref.1) | copy-start | bytes 49156
  3.6 28.8 %copy-start.3 = (s32[64,64,1]{1,2,0:T(1,128)S(1)}, s32[64,64,1]{1,2,0:T(1,128)}, u32[]{:S(2)}) copy-start(s32[64,64,1]{1,2,0:T(1,128)} %param.12) | copy-start | bytes 49156

commit v3 on v2

--- a/solution.py
+++ b/solution.py
@@ -30,6 +30,24 @@
         ],
         0,
     ).astype(jnp.bfloat16)
+
+
+def partner(me, step, count):
+    if count & (count - 1):
+        return lax.rem(me + step, count)
+    found, bit = 0, 1
+    while bit < count:
+        mine = lax.rem(me // bit, 2)
+        flip = lax.rem(step // bit, 2) if not isinstance(step, int) else step // bit % 2
+        found = found + bit * (mine + flip - 2 * mine * flip)
+        bit *= 2
+    return found
+
+
+def partner_back(me, step, count):
+    if count & (count - 1):
+        return lax.rem(me + count - step, count)
+    return partner(me, step, count)
 
 
 def products_kernel(
@@ -56,8 +74,8 @@
     peers = lax.axis_size("panel")
     me = lax.axis_index("panel")
     turn = pl.program_id(0)
-    offset = turn // own + 1
-    peer = lax.rem(me + offset, peers)
+    offset = peers - 1 - turn // own
+    peer = partner(me, offset, peers)
     part = lax.rem(turn, own)
     barrier = pltpu.get_barrier_semaphore()
 
@@ -77,7 +95,7 @@
             pl.semaphore_signal(
                 barrier,
                 inc=1,
-                device_id={"panel": lax.rem(me + step, peers)},
+                device_id={"panel": partner(me, step, peers)},
                 device_id_type=pl.DeviceIdType.MESH,
             )
         block = (
@@ -91,6 +109,7 @@
                 hit = hit | (names[k][:, n : n + 1] == block)
             masks[:, n * stack : (n + 1) * stack] = jnp.where(hit, 1.0, 0.0)
 
+    cut = res // 128 * 128
     lane = lax.broadcasted_iota(jnp.int32, (layers, stack), 1)
     sign = jnp.where(lane < antennas, -1.0, 1.0)
     mask = masks[pl.ds(peer * own + part, 1), :]
@@ -104,21 +123,32 @@
             jnp.bfloat16
         )
         right[n * stack : (n + 1) * stack, :] = beams
-        cut = res // 128 * 128
         turned = beams[:, cut:].T[res - cut :].astype(jnp.float32)
         turned = turned * mask[:, n * stack : (n + 1) * stack]
         swapped = pltpu.roll(turned, antennas, 1) * sign
         left[:layers, n * stack : (n + 1) * stack] = turned.astype(jnp.bfloat16)
         left[layers:, n * stack : (n + 1) * stack] = swapped.astype(jnp.bfloat16)
-    sent[peer, part] = jnp.dot(
-        left[...], right[...], preferred_element_type=jnp.float32
-    ).astype(sent.dtype)
+    result = jnp.dot(left[...], right[...], preferred_element_type=jnp.float32)
+    off = res - cut
+    filler = jnp.zeros((layers, cut + 128 - layers - res), jnp.float32)
+    real = jnp.concatenate([result[:layers, cut:], filler], 1)
+    imag = jnp.concatenate([result[layers:, cut:], filler], 1)
+    row_id = lax.broadcasted_iota(jnp.int32, (layers, 128), 0)
+    lane_id = lax.broadcasted_iota(jnp.int32, (layers, 128), 1)
+    mixed = jnp.where(
+        lane_id >= off + layers,
+        pltpu.roll(imag, off + layers, 1),
+        jnp.where(row_id + off < lane_id, imag, real),
+    )
+    sent[peer, part, :, :cut] = result[:layers, :cut].astype(sent.dtype)
+    sent[peer, part, :, cut : 2 * cut] = result[layers:, :cut].astype(sent.dtype)
+    sent[peer, part, :, 2 * cut :] = mixed.astype(sent.dtype)
 
     @pl.when(turn == 0)
     def _():
         pl.semaphore_wait(barrier, peers - 1)
 
-    @pl.when(offset < peers)
+    @pl.when(offset > 0)
     def _():
         copy(peer, me, part).start()
 
@@ -127,13 +157,13 @@
         for j in range(own):
             total = sent[me, j].astype(jnp.float32)
             for step in range(1, peers):
-                source = lax.rem(me + peers - step, peers)
+                source = partner_back(me, peers - step, peers)
                 copy(source, source, j).wait_recv()
                 total = total + held[source, j].astype(jnp.float32)
             out_ref[j] = total
         for j in range(own):
             for step in range(1, peers):
-                there = lax.rem(me + step, peers)
+                there = partner(me, peers - step, peers)
                 copy(there, me, j).wait_send()
 
 
@@ -157,7 +187,6 @@
     own = parts_ref.shape[0]
     users = noise_ref.shape[1]
     rows = own * layers
-    width = layers + res
     cut = res // 128 * 128
     off = res - cut
     prbs = lax.axis_size("prb")
@@ -209,13 +238,25 @@
             ],
             1,
         )
-        re[p, :, :cut] = total[:layers, :cut]
-        im[p, :, :cut] = total[layers:, :cut]
-        filler = jnp.zeros((layers, cut + 128 - width), jnp.float32)
-        re[p, :, cut:] = jnp.concatenate([total[:layers, cut:], filler], 1) + jnp.where(
-            row_id + off == lane_id, spread, 0.0
-        )
-        im[p, :, cut:] = jnp.concatenate([total[layers:, cut:], filler], 1)
+        re[p, :, :cut] = total[:, :cut]
+        im[p, :, :cut] = total[:, cut : 2 * cut]
+        mixed = total[:, 2 * cut :]
+        turned = jnp.concatenate([mixed, jnp.zeros((128 - layers, 128), jnp.float32)], 0).T
+        turned = pltpu.roll(turned[off : off + layers], off, 1)
+        re[p, :, cut:] = jnp.where(
+            row_id + off < lane_id,
+            turned,
+            jnp.where(row_id + off == lane_id, mixed + spread, mixed),
+        )
+        im[p, :, cut:] = jnp.where(
+            lane_id < off,
+            pltpu.roll(mixed, 128 - off - layers, 1),
+            jnp.where(
+                row_id + off < lane_id,
+                mixed,
+                jnp.where(row_id + off == lane_id, 0.0, -turned),
+            ),
+        )
         owners.append(owner_ref[pl.ds(first + p, 1), :])
 
     def wide(x):
@@ -322,15 +363,16 @@
     slots = -(-capacity // 8) * 8
     stack = 2 * antennas
     width = layers + res
+    packed = 2 * (res // 128 * 128) + 128
     kmax = keep_list.shape[-1]
 
     def prb_of(turn):
-        peer = lax.rem(lax.axis_index("panel") + turn // own + 1, peers)
+        peer = partner(lax.axis_index("panel"), peers - 1 - turn // own, peers)
         return peer * own + lax.rem(turn, own)
 
     totals = pl.pallas_call(
         functools.partial(products_kernel, layers, res, own),
-        out_shape=jax.ShapeDtypeStruct((own, 2 * layers, width), jnp.float32),
+        out_shape=jax.ShapeDtypeStruct((own, layers, packed), jnp.float32),
         grid=(prb_local,),
         in_specs=[
             pl.BlockSpec((panels, 1, antennas, 2 * layers), lambda t: (0, prb_of(t), 0, 0)),
@@ -338,18 +380,18 @@
             pl.BlockSpec((kmax, panels, prb_local), lambda t: (0, 0, 0)),
             pl.BlockSpec((stack, stack), lambda t: (0, 0)),
         ],
-        out_specs=pl.BlockSpec((own, 2 * layers, width), lambda t: (0, 0, 0)),
+        out_specs=pl.BlockSpec((own, layers, packed), lambda t: (0, 0, 0)),
         scratch_shapes=[
             pltpu.VMEM((2 * layers, panels * stack), jnp.bfloat16),
             pltpu.VMEM((panels * stack, width), jnp.bfloat16),
             pltpu.VMEM((prb_local, panels * stack), jnp.float32),
-            pltpu.VMEM((peers, own, 2 * layers, width), jnp.bfloat16),
-            pltpu.VMEM((peers, own, 2 * layers, width), jnp.bfloat16),
+            pltpu.VMEM((peers, own, layers, packed), jnp.bfloat16),
+            pltpu.VMEM((peers, own, layers, packed), jnp.bfloat16),
             pltpu.SemaphoreType.DMA((peers, own)),
             pltpu.SemaphoreType.DMA((peers, own)),
         ],
         compiler_params=pltpu.CompilerParams(
-            vmem_limit_bytes=48 << 20, collective_id=0, has_side_effects=True
+            vmem_limit_bytes=63 << 20, collective_id=0, has_side_effects=True
         ),
     )(channel, received, jnp.transpose(keep_list, (2, 0, 1)), table)
 

time: 54.1 us -> 44.2 us (0.82)
  Pallas kernels: 49.1 us -> 42.1 us
  local copies, waits for them, and re-layouts: 4.41 us -> 1.79 us
    pallas_call x1, Pallas kernels: 20.3 us -> 13.8 us  [body(): pl.pallas_call(functools.partial(solve_kernel, layers, res, capacity, slo...]
    unnamed x12 -> x8, local copies, waits for them, and re-layouts: 3.56 us -> 0.93 us
where the time goes in v3:
time: 44.2 us; the launch traced here: 43.9 us
  Pallas kernels  42.1 us (95%)
  local copies, waits for them, and re-layouts  1.79 us (4%)
    pallas_call x1, Pallas kernels, body(): pl.pallas_call(functools.partial(products_kernel, layers, res, own), out_...  28.3 us
    pallas_call x1, Pallas kernels, body(): pl.pallas_call(functools.partial(solve_kernel, layers, res, capacity, slo...  13.8 us
    unnamed x8, local copies, waits for them, and re-layouts  0.93 us

profile of v3, /device:TPU:0, one launch (start us, length us, event | category | flops | bytes accessed | tf_op | source)
XLA Modules:
  0.0 43.9 jit_solution(11306678129817038211)
XLA Ops:
  0.0 0.0 copy-start.2
  0.0 0.0 copy-start.3
  0.0 0.0 copy-start.1
  0.0 28.3 %shard_map.73.parts_ref = f32[2,64,384]{2,1,0:T(8,128)} custom-call(bf16[14,16,64,128]{3,2,1,0:T(8,128)(2,1)} %h_ref.1, bf16[14,16,64,288]{3,2,1,0:T(8,128)(2,1)} %y_ref.1, s32[3,14,16]{2,1,0:T(8,128)} %bitcast.5, bf16[128,128]{1,0:T(8,128)(2,1)} %constant.2.clone.f_ref), custom_call_target="tpu_custom_call" | custom-call | tf_op jit(solution)/shard_map/pallas_call | solution.py:373
  28.3 0.0 copy-done.2
  28.3 0.0 copy-done.3
  28.3 0.0 copy-done.1
  28.3 0.0 copy-start
  28.3 0.9 %copy-done = f32[2,64,384]{2,1,0:T(8,128)S(1)} copy-done((f32[2,64,384]{2,1,0:T(8,128)S(1)}, f32[2,64,384]{2,1,0:T(8,128)}, u32[]{:S(2)}) %copy-start) | copy-done | bytes 196632
  29.3 13.8 %shard_map.74 = f32[256,288]{1,0:T(8,128)S(1)} custom-call(f32[2,64,384]{2,1,0:T(8,128)S(1)} %copy-done, s32[64,64]{1,0:T(8,128)S(1)} %copy-done.1, f32[1,512]{1,0:T(1,128)S(1)} %bitcast.4, s32[64,64]{1,0:T(8,128)S(1)} %bitcast.3), custom_call_target="tpu_custom_call" | custom-call | tf_op jit(solution)/shard_map/pallas_call | solution.py:398
  43.1 0.9 %copy.8 = f32[256,288]{0,1:T(8,128)} copy(f32[256,288]{1,0:T(8,128)S(1)} %shard_map.74) | data formatting | bytes 589824 | tf_op jit(solution)/shard_map/pallas_call | solution.py:398
Async XLA Ops:
  0.0 28.3 %copy-start.2 = (s32[64,64,1]{1,2,0:T(1,128)S(1)}, s32[64,64,1]{1,2,0:T(1,128)}, u32[]{:S(2)}) copy-start(s32[64,64,1]{1,2,0:T(1,128)} %param.12) | copy-start | bytes 49156
  0.0 28.3 %copy-start.3 = (f32[512]{0:T(512)S(1)}, f32[512]{0:T(512)}, u32[]{:S(2)}) copy-start(f32[512]{0:T(512)} %param.11) | copy-start | bytes 6148
  0.0 28.3 %copy-start.1 = (s32[64,64]{1,0:T(8,128)S(1)}, s32[64,64]{1,0:T(8,128)}, u32[]{:S(2)}) copy-start(s32[64,64]{1,0:T(8,128)} %alloc_ref.1) | copy-start | bytes 49156
  28.3 0.9 %copy-start = (f32[2,64,384]{2,1,0:T(8,128)S(1)}, f32[2,64,384]{2,1,0:T(8,128)}, u32[]{:S(2)}) copy-start(f32[2,64,384]{2,1,0:T(8,128)} %shard_map.73.parts_ref) | copy-start | bytes 589828

commit v4 on v3

--- a/solution.py
+++ b/solution.py
@@ -11,6 +11,7 @@
 
 ANTENNA_EDGE = 8
 NBLK = 4
+GROUP = 4
 
 
 def beam_matrix(panel_side):
@@ -113,6 +114,8 @@
     lane = lax.broadcasted_iota(jnp.int32, (layers, stack), 1)
     sign = jnp.where(lane < antennas, -1.0, 1.0)
     mask = masks[pl.ds(peer * own + part, 1), :]
+    result = None
+    done = 0
     for n in range(panels):
         h = h_ref[n, 0]
         y = y_ref[n, 0]
@@ -128,7 +131,11 @@
         swapped = pltpu.roll(turned, antennas, 1) * sign
         left[:layers, n * stack : (n + 1) * stack] = turned.astype(jnp.bfloat16)
         left[layers:, n * stack : (n + 1) * stack] = swapped.astype(jnp.bfloat16)
-    result = jnp.dot(left[...], right[...], preferred_element_type=jnp.float32)
+        if n % GROUP == GROUP - 1 or n == panels - 1:
+            here = slice(done * stack, (n + 1) * stack)
+            term = jnp.dot(left[:, here], right[here, :], preferred_element_type=jnp.float32)
+            result = term if result is None else result + term
+            done = n + 1
     off = res - cut
     filler = jnp.zeros((layers, cut + 128 - layers - res), jnp.float32)
     real = jnp.concatenate([result[:layers, cut:], filler], 1)

time: 44.2 us -> 44.5 us (level)
  no operation moved by 1% of the time
where the time goes in v4:
time: 44.5 us; the launch traced here: 44.1 us
  Pallas kernels  42.3 us (95%)
  local copies, waits for them, and re-layouts  1.79 us (4%)
    pallas_call x1, Pallas kernels, body(): pl.pallas_call(functools.partial(products_kernel, layers, res, own), out_...  28.5 us
    pallas_call x1, Pallas kernels, body(): pl.pallas_call(functools.partial(solve_kernel, layers, res, capacity, slo...  13.8 us
    unnamed x8, local copies, waits for them, and re-layouts  0.93 us

profile of v4, /device:TPU:0, one launch (start us, length us, event | category | flops | bytes accessed | tf_op | source)
XLA Modules:
  0.0 44.1 jit_solution(12358752381947399294)
XLA Ops:
  0.0 0.0 copy-start.2
  0.0 0.0 copy-start.3
  0.0 0.0 copy-start.1
  0.0 28.5 %shard_map.73.parts_ref = f32[2,64,384]{2,1,0:T(8,128)} custom-call(bf16[14,16,64,128]{3,2,1,0:T(8,128)(2,1)} %h_ref.1, bf16[14,16,64,288]{3,2,1,0:T(8,128)(2,1)} %y_ref.1, s32[3,14,16]{2,1,0:T(8,128)} %bitcast.5, bf16[128,128]{1,0:T(8,128)(2,1)} %constant.2.clone.f_ref), custom_call_target="tpu_custom_call" | custom-call | tf_op jit(solution)/shard_map/pallas_call | solution.py:380
  28.5 0.0 copy-done.2
  28.5 0.0 copy-done.3
  28.5 0.0 copy-done.1
  28.6 0.0 copy-start
  28.6 0.9 %copy-done = f32[2,64,384]{2,1,0:T(8,128)S(1)} copy-done((f32[2,64,384]{2,1,0:T(8,128)S(1)}, f32[2,64,384]{2,1,0:T(8,128)}, u32[]{:S(2)}) %copy-start) | copy-done | bytes 196632
  29.5 13.8 %shard_map.74 = f32[256,288]{1,0:T(8,128)S(1)} custom-call(f32[2,64,384]{2,1,0:T(8,128)S(1)} %copy-done, s32[64,64]{1,0:T(8,128)S(1)} %copy-done.1, f32[1,512]{1,0:T(1,128)S(1)} %bitcast.4, s32[64,64]{1,0:T(8,128)S(1)} %bitcast.3), custom_call_target="tpu_custom_call" | custom-call | tf_op jit(solution)/shard_map/pallas_call | solution.py:405
  43.3 0.9 %copy.8 = f32[256,288]{0,1:T(8,128)} copy(f32[256,288]{1,0:T(8,128)S(1)} %shard_map.74) | data formatting | bytes 589824 | tf_op jit(solution)/shard_map/pallas_call | solution.py:405
Async XLA Ops:
  0.0 28.5 %copy-start.2 = (s32[64,64,1]{1,2,0:T(1,128)S(1)}, s32[64,64,1]{1,2,0:T(1,128)}, u32[]{:S(2)}) copy-start(s32[64,64,1]{1,2,0:T(1,128)} %param.12) | copy-start | bytes 49156
  0.0 28.5 %copy-start.3 = (f32[512]{0:T(512)S(1)}, f32[512]{0:T(512)}, u32[]{:S(2)}) copy-start(f32[512]{0:T(512)} %param.11) | copy-start | bytes 6148
  0.0 28.5 %copy-start.1 = (s32[64,64]{1,0:T(8,128)S(1)}, s32[64,64]{1,0:T(8,128)}, u32[]{:S(2)}) copy-start(s32[64,64]{1,0:T(8,128)} %alloc_ref.1) | copy-start | bytes 49156
  28.6 0.9 %copy-start = (f32[2,64,384]{2,1,0:T(8,128)S(1)}, f32[2,64,384]{2,1,0:T(8,128)}, u32[]{:S(2)}) copy-start(f32[2,64,384]{2,1,0:T(8,128)} %shard_map.73.parts_ref) | copy-start | bytes 589828
